TPU v7x, 32 devices: a whole 2x2x4 slice. The times are simulated.
32 devices in a mesh: dp: 8 (over z, x), tensor: 4 (over y, core).
Axes of the slice: x: 2, y: 2, z: 4, core: 2. Of those that a mesh axis runs over, the one named last changes fastest.
Arguments:
- tokens: bfloat16 [14336, 1024], P('dp'), may hold values from -6 to 6
- lengths: int32 [8, 8], P('dp'), may hold values from 0 to 1568, as said below
- owner: int32 [8], replicated, may hold values from 0 to 7, each once
- attend_master: float32 [3, 1024, 1024], P(None, 'dp', 'tensor'), may hold values from -0.1875 to 0.1875
- attend_first: float32 [3, 1024, 1024], P(None, 'dp', 'tensor'), may hold values from -40 to 40
- attend_second: float32 [3, 1024, 1024], P(None, 'dp', 'tensor'), may hold values from 189.2352 to 759.808
- output_master: float32 [1024, 1024], P('dp', 'tensor'), may hold values from -1.5 to 1.5
- output_first: float32 [1024, 1024], P('dp', 'tensor'), may hold values from -6 to 6
- output_second: float32 [1024, 1024], P('dp', 'tensor'), may hold values from 17.2032 to 68.8128
- dense_master: float32 [2, 1024, 4, 1024], P(None, 'dp', None, 'tensor'), may hold values from -0.1875 to 0.1875
- dense_first: float32 [2, 1024, 4, 1024], P(None, 'dp', None, 'tensor'), may hold values from -40 to 40
- dense_second: float32 [2, 1024, 4, 1024], P(None, 'dp', None, 'tensor'), may hold values from 189.2352 to 759.808
- bias_master: float32 [5, 1024], P(None, ('tensor', 'dp')), may hold values from -1.2 to 1.2
- bias_first: float32 [5, 1024], P(None, ('tensor', 'dp')), may hold values from -32 to 32
- bias_second: float32 [5, 1024], P(None, ('tensor', 'dp')), may hold values from 143.36 to 573.44
- vector_master: float32 [6, 1024], P(None, 'dp'), may hold values from -1.2 to 1.6, as said below
- vector_first: float32 [6, 1024], P(None, 'dp'), may hold values from -80 to 80
- vector_second: float32 [6, 1024], P(None, 'dp'), may hold values from 759.808 to 3010.56
- cotangent: bfloat16 [14336, 1024], P('dp'), may hold values from -6 to 6
Outputs:
- layer_output: bfloat16 [14336, 1024], P('dp')
- tokens_grad: bfloat16 [14336, 1024], P('dp')
- attend_first_next: float32 [3, 1024, 1024], P(None, 'dp', 'tensor')
- attend_second_next: float32 [3, 1024, 1024], P(None, 'dp', 'tensor')
- attend_updated: float32 [3, 1024, 1024], P(None, 'dp', 'tensor')
- output_first_next: float32 [1024, 1024], P('dp', 'tensor')
- output_second_next: float32 [1024, 1024], P('dp', 'tensor')
- output_updated: float32 [1024, 1024], P('dp', 'tensor')
- dense_first_next: float32 [2, 1024, 4, 1024], P(None, 'dp', None, 'tensor')
- dense_second_next: float32 [2, 1024, 4, 1024], P(None, 'dp', None, 'tensor')
- dense_updated: float32 [2, 1024, 4, 1024], P(None, 'dp', None, 'tensor')
- bias_first_next: float32 [5, 1024], P(None, ('tensor', 'dp'))
- bias_second_next: float32 [5, 1024], P(None, ('tensor', 'dp'))
- bias_updated: float32 [5, 1024], P(None, ('tensor', 'dp'))
- vector_first_next: float32 [6, 1024], P(None, 'dp')
- vector_second_next: float32 [6, 1024], P(None, 'dp')
- vector_updated: float32 [6, 1024], P(None, 'dp')
Inputs may be any that keep to these rules, and one draw needn't show every extreme that they name: `lengths`: each row lists the sequences packed in order onto that dp index's 1792 rows; an entry is 0 (an empty slot) or a multiple of 196, at most one entry of a row exceeds 196, a row sums to at most 1792, and some dp index holds a sequence of exactly 1568 tokens. `owner`: each number of 0 to 7 appears once. `vector_master`: rows 2 and 4 are norms' gains near one; the other rows are biases of both signs.
All inputs are finite; a program needn't handle non-finite values.
Results may differ from a plain program's by a relative error of at most 0.025.
Values may be sent and summed in bfloat16 or wider, within the bound.
A program may use at most 256 MiB of HBM per device.

v0:
```python
import functools

import jax
import jax.numpy as jnp
from jax import lax
from jax.experimental import pallas as pl
from jax.experimental.pallas import tpu as pltpu
from jax.sharding import PartitionSpec as P

HD = 64
STEP = 10
LANES = 128
BLOCK = 256
MESH = pl.DeviceIdType.MESH
BIG = 2.0**50

norm_epsilon = 1e-06
first_decay = 0.9
second_decay = 0.95
adam_epsilon = 1e-08
matrix_rate = 0.1
output_rate = 0.5
bias_rate = 0.5
vector_rate = 1.0
matrix_decay = 0.05

half_type = jnp.bfloat16
full_type = jnp.float32


def dot(left, right, left_dim=1, right_dim=0):
    return lax.dot_general(
        left, right, (((left_dim,), (right_dim,)), ((), ())), preferred_element_type=full_type
    )


def ring_pos(place, count):
    column = place % 2
    row = place // 2
    return row * (1 - column) + (count - 1 - row) * column


def ring_at(pos, count):
    near = (pos + 2 * count) % count
    down = near // (count // 2)
    return 2 * near * (1 - down) + (2 * count - 1 - 2 * near) * down


def normalized(x):
    center = jnp.mean(x, axis=-1, keepdims=True)
    offset = x - center
    spread = jnp.mean(offset * offset, axis=-1, keepdims=True)
    rate = lax.rsqrt(spread + norm_epsilon)
    return offset * rate, rate


class Gather:
    def __init__(self, view, width, sems, count):
        self.view, self.width, self.sems, self.count = view, width, sems, count
        self.steps = count // 2
        self.pos = ring_pos(lax.axis_index("dp"), count)
        self.tensor = lax.axis_index("tensor")

    def _copy(self, way, step, hops):
        sign = 1 - 2 * way
        part = (0, self.width)
        if step == self.steps - 1:
            part = (way * (self.width // 2), self.width // 2)
        block = self.view(ring_at(self.pos - sign * hops, self.count), *part)
        return pltpu.make_async_remote_copy(
            src_ref=block,
            dst_ref=block,
            send_sem=self.sems.at[2 * way, step],
            recv_sem=self.sems.at[2 * way + 1, step],
            device_id=(ring_at(self.pos + sign, self.count), self.tensor),
            device_id_type=MESH,
        )

    def advance(self, step):
        if step:
            for way in range(2):
                self._copy(way, step - 1, step).wait_recv()
        if step < self.steps:
            for way in range(2):
                self._copy(way, step, step).start()

    def sent(self):
        for step in range(self.steps):
            for way in range(2):
                self._copy(way, step, step).wait_send()


class RowSum:
    def __init__(self, term, given, sent, crossed, sems):
        self.term, self.given, self.sent_ref, self.crossed = term, given, sent, crossed
        self.slots, self.sent_slots, self.blocks = term.shape[0], sent.shape[0], given.shape[0]
        self.sems = sems
        self.half = given.shape[1]
        self.dp, tensor = lax.axis_index("dp"), lax.axis_index("tensor")
        self.core = tensor % 2
        self.mate = tensor - tensor % 2 + (tensor + 1) % 2
        self.other = (tensor + 2) % 4

    def rows(self, core):
        return pl.ds(pl.multiple_of(core * self.half, self.half), self.half)

    def _give(self, i):
        return pltpu.make_async_remote_copy(
            src_ref=self.term.at[i % self.slots, self.rows(1 - self.core), :],
            dst_ref=self.given.at[i],
            send_sem=self.sems.at[0, i],
            recv_sem=self.sems.at[1, i],
            device_id=(self.dp, self.mate),
            device_id_type=MESH,
        )

    def _cross(self, i):
        return pltpu.make_async_remote_copy(
            src_ref=self.sent_ref.at[i % self.sent_slots],
            dst_ref=self.crossed.at[i],
            send_sem=self.sems.at[2, i],
            recv_sem=self.sems.at[3, i],
            device_id=(self.dp, self.other),
            device_id_type=MESH,
        )

    def free(self, i):
        if self.slots < self.blocks:

            @pl.when(i >= self.slots)
            def _():
                self._give(i - self.slots).wait_send()

    def give(self, i):
        self._give(i).start()

    def cross(self, i):
        self._give(i).wait_recv()
        mine = self.term[i % self.slots, self.rows(self.core), :].astype(full_type)
        if self.sent_slots < self.blocks:

            @pl.when(i >= self.sent_slots)
            def _():
                self._cross(i - self.sent_slots).wait_send()

        total = mine + self.given[i].astype(full_type)
        self.sent_ref[i % self.sent_slots] = total.astype(half_type)
        self._cross(i).start()

    def total(self, i):
        self._cross(i).wait_recv()
        mine = self.sent_ref[i % self.sent_slots].astype(full_type)
        return mine + self.crossed[i].astype(full_type)

    def gone(self):
        def given(i, carry):
            self._give(i).wait_send()
            return carry

        lax.fori_loop(max(self.blocks - self.slots, 0), self.blocks, given, 0)

    def finish(self, given=True):
        if given:
            self.gone()

        def crossed(i, carry):
            self._cross(i).wait_send()
            return carry

        lax.fori_loop(max(self.blocks - self.sent_slots, 0), self.blocks, crossed, 0)


class Share:
    def __init__(self, ref, sems):
        self.ref, self.sems = ref, sems
        self.dp, tensor = lax.axis_index("dp"), lax.axis_index("tensor")
        self.core = tensor % 2
        self.mate = tensor - tensor % 2 + (tensor + 1) % 2

    def rows(self, i, core):
        half = BLOCK // 2
        return pl.ds(pl.multiple_of(i * BLOCK + core * half, half), half)

    def _copy(self, i, core):
        piece = self.ref.at[self.rows(i, core), :]
        return pltpu.make_async_remote_copy(
            src_ref=piece,
            dst_ref=piece,
            send_sem=self.sems.at[0, i],
            recv_sem=self.sems.at[1, i],
            device_id=(self.dp, self.mate),
            device_id_type=MESH,
        )

    def put(self, i, value):
        self.ref[self.rows(i, self.core), :] = value
        self._copy(i, self.core).start()

    def arrived(self, i):
        self._copy(i, 1 - self.core).wait_recv()

    def finish(self, blocks):
        def done(i, carry):
            self._copy(i, self.core).wait_send()
            return carry

        lax.fori_loop(0, blocks, done, 0)


def greet(peers):
    barrier = pltpu.get_barrier_semaphore()
    for peer in peers:
        pl.semaphore_signal(barrier, inc=1, device_id=peer, device_id_type=MESH)
    return lambda: pl.semaphore_wait(barrier, len(peers))


def tensor_peers():
    dp, tensor = lax.axis_index("dp"), lax.axis_index("tensor")
    return [(dp, tensor - tensor % 2 + (tensor + 1) % 2), (dp, (tensor + 2) % 4)]


def ring_peers(count):
    dp, tensor = lax.axis_index("dp"), lax.axis_index("tensor")
    pos = ring_pos(dp, count)
    return [(ring_at(pos + 1, count), tensor), (ring_at(pos - 1, count), tensor)]


def dp_peers(count):
    dp, tensor = lax.axis_index("dp"), lax.axis_index("tensor")
    return [((dp + k) % count, tensor) for k in range(1, count)]


def three_parts(x):
    high = x.astype(half_type).astype(full_type)
    middle = (x - high).astype(half_type).astype(full_type)
    return high, middle, x - high - middle


def gelu_parts(z):
    phi = 0.5 + 0.5 * lax.erf(z * (0.5**0.5))
    slope = phi + z * (jnp.exp(-0.5 * z * z) * (2.0 * 3.141592653589793) ** -0.5)
    return z * phi, slope


def fetch(source, target, sems):
    def copy(i):
        rows = pl.ds(pl.multiple_of(i * BLOCK, BLOCK), BLOCK)
        return pltpu.make_async_copy(source.at[rows, :], target.at[rows, :], sems.at[i])

    return copy


def stored_order(x, owner_ref):
    count = owner_ref.shape[0]
    wide = x.shape[1] // count
    if wide % LANES:
        return x
    parts = []
    for j in range(count):
        total = None
        for n in range(count):
            term = x[:, n * wide : (n + 1) * wide] * jnp.where(owner_ref[j] == n, 1.0, 0.0)
            total = term if total is None else total + term
        parts.append(total)
    return jnp.concatenate(parts, axis=1)


def front_kernel(
    count, len_ref, owner_ref, tok_hbm, cot_hbm, att_ref, out_ref, dense_ref, vector_ref, split_ref,
    a1_hbm, ga_hbm, h2_hbm, own_hbm, qa_hbm, ka_hbm, va_hbm, o_hbm, w_hbm, gh2_hbm, down_hbm,
    up_hbm, dn_hbm, goa_hbm, kt_hbm, vec_ref, gbias_ref, gvec_ref,
    own_ref, qa_ref, ka_ref, va_ref, o_ref, w_ref, wo_ref, gh2_ref, down_ref, ul_ref, gz_ref, made,
    norm_ref, cot_ref, wd_ref, ga_ref, goa_ref, kt_ref, bias_ref, b1_ref, small_ref, smalls,
    mixed_ref, term2, given2, sent2, crossed2,
    gather_sems, small_sems, spread_sems, mixed_sems, sum2_sems, share_sems, put_sems, local_sems,
    whole_sems, made_sems,
):
    me, tensor = lax.axis_index("dp"), lax.axis_index("tensor")
    total_rows, width = norm_ref.shape
    local_width = out_ref.shape[1]
    ratio = dense_ref.shape[2]
    wide = width // count
    slots = len_ref.shape[1]
    heads = local_width // HD
    blocks = total_rows // BLOCK
    half = BLOCK // 2
    lanes = small_ref.shape[1] - local_width
    fold = lanes // wide
    steps = count // 2
    core = tensor % 2
    mate = tensor - core + 1 - core
    other, across = (tensor + 2) % 4, (mate + 2) % 4

    greeted = greet(tensor_peers() + [(me, across)] + dp_peers(count))
    tokens_in = fetch(tok_hbm, norm_ref, local_sems.at[0])
    cot_in = fetch(cot_hbm, cot_ref, local_sems.at[1])
    a1_out = fetch(norm_ref, a1_hbm, local_sems.at[2])
    for i in range(blocks):
        tokens_in(i).start()
    for i in range(blocks):
        cot_in(i).start()
    mine = pl.ds(pl.multiple_of(me * wide, wide), wide)
    for row in range(3):
        w_ref[mine, row * local_width : (row + 1) * local_width] = att_ref[row].astype(half_type)

    def columns_of(index, low=0, size=local_width):
        return pl.ds(pl.multiple_of(index * local_width + low, LANES), size)

    wo_ref[mine, columns_of(tensor)] = out_ref[...].astype(half_type)

    small_ref[...] = jnp.zeros_like(small_ref)
    vectors = vector_ref[...].astype(half_type)
    if fold == 1:
        small_ref[0:6, :lanes] = vectors.astype(full_type)
    else:
        row = lax.broadcasted_iota(jnp.int32, (wide, lanes), 0)
        column = lax.broadcasted_iota(jnp.int32, (wide, lanes), 1)
        spread = jnp.where(column == row + me % fold * wide, 1.0, 0.0).astype(half_type)
        small_ref[0:6, :lanes] = dot(vectors, spread)
    narrow = split_ref.shape[1]
    row = lax.broadcasted_iota(jnp.int32, (narrow, local_width), 0)
    column = lax.broadcasted_iota(jnp.int32, (narrow, local_width), 1)
    spread = jnp.where(column == row + owner_ref[me] * narrow, 1.0, 0.0).astype(half_type)
    small_ref[0 : 1 + ratio, lanes:] = dot(split_ref[...].astype(half_type), spread)
    smalls[me] = small_ref[...]
    greeted()

    def place(block):
        return pl.ds(pl.multiple_of(block * wide, wide), wide)

    def small_copy(source, peer):
        return pltpu.make_async_remote_copy(
            src_ref=small_ref,
            dst_ref=smalls.at[source],
            send_sem=small_sems.at[0, peer],
            recv_sem=small_sems.at[1, source],
            device_id=(peer, tensor),
            device_id_type=MESH,
        )

    def send_small(k, carry):
        small_copy(me, (me + k) % count).start()
        return carry

    lax.fori_loop(1, count, send_small, 0)

    def attend_view(row):
        return lambda block, low, size: w_ref.at[
            place(block), pl.ds(row * local_width + low, size)
        ]

    def dense_view(row):
        return lambda block, low, size: wd_ref.at[row, place(block), pl.ds(low, size)]

    attend = [Gather(attend_view(row), local_width, gather_sems.at[row], count) for row in range(3)]
    attend.append(
        Gather(
            lambda block, low, size: wo_ref.at[place(block), columns_of(tensor, low, size)],
            local_width, gather_sems.at[3], count,
        )
    )
    dense = [
        Gather(dense_view(row), ratio * local_width, gather_sems.at[4 + row], count)
        for row in range(2)
    ]
    for piece in attend:
        piece.advance(0)

    def spread(kind, block, source, target):
        piece = wo_ref.at[place(block), columns_of(source)]
        return pltpu.make_async_remote_copy(
            src_ref=piece,
            dst_ref=piece,
            send_sem=spread_sems.at[2 * kind, block],
            recv_sem=spread_sems.at[2 * kind + 1, block],
            device_id=(me, target),
            device_id_type=MESH,
        )

    def spread_step(step):
        pos = attend[3].pos
        hops = {0: [0], steps: [steps]}.get(step, [step, -step])
        for hop in hops:
            block = ring_at(pos - hop, count)
            spread(0, block, tensor, mate).start()
            spread(1, block, tensor, other).start()

    spread_step(0)
    for row in range(2):
        for r in range(ratio):
            wd_ref[row, mine, r * local_width : (r + 1) * local_width] = dense_ref[
                row, :, r, :
            ].astype(half_type)

    def take_small(k, carry):
        source = (me + k) % count
        small_copy(source, source).wait_recv()
        return carry

    lax.fori_loop(1, count, take_small, 0)
    bias = smalls[0, :, lanes:]
    for j in range(1, count):
        bias = bias + smalls[j, :, lanes:]
    bias_ref[...] = bias
    for r in range(ratio):
        b1_ref[:, r * local_width : (r + 1) * local_width] = bias[1 + r : 2 + r, :]
    for window in range(width // lanes):
        piece = smalls[window * fold, :, :lanes]
        for j in range(window * fold + 1, (window + 1) * fold):
            piece = piece + smalls[j, :, :lanes]
        vec_ref[:, window * lanes : (window + 1) * lanes] = piece

    def norm_rows(i, carry):
        tokens_in(i).wait()
        rows = pl.ds(pl.multiple_of(i * BLOCK, BLOCK), BLOCK)
        x = stored_order(norm_ref[rows, :].astype(full_type), owner_ref)
        norm_ref[rows, :] = x.astype(half_type)
        here = pl.ds(pl.multiple_of(i * BLOCK + core * half, half), half)
        own_ref[pl.ds(pl.multiple_of(i * half, half), half), :] = norm_ref[here, :]
        unit, _ = normalized(x)
        norm_ref[rows, :] = (unit * vec_ref[2:3, :] + vec_ref[3:4, :]).astype(half_type)
        a1_out(i).start()
        cot_in(i).wait()
        cot_ref[rows, :] = stored_order(cot_ref[rows, :].astype(full_type), owner_ref).astype(
            half_type
        )
        return carry

    done = 0
    for step in range(1, steps + 1):
        for piece in attend:
            piece.advance(step)
        spread_step(step)
        if step == steps - 1:
            for piece in dense:
                piece.advance(0)
        upto = min(blocks, -(-blocks * step // (steps - 1)))
        if upto > done:
            lax.fori_loop(done, upto, norm_rows, 0)
        done = max(done, upto)

    pumps = [(piece, step) for step in range(1, steps + 1) for piece in dense]

    def pump(slot):
        for k, (piece, step) in enumerate(pumps):
            if min(blocks + 1, (13 * k + 2) // 10 * 8 // len(pumps)) == slot:
                piece.advance(step)

    lane = lax.broadcasted_iota(jnp.int32, (BLOCK, LANES), 1)
    low_half = lane < HD
    spot = lane % HD

    def project(i, carry):
        row = pl.multiple_of(i * BLOCK, BLOCK)
        rows = pl.ds(row, BLOCK)
        a1 = norm_ref[rows, :]
        qkv = dot(a1, w_ref[...])
        q, k, v = (qkv[:, part * local_width : (part + 1) * local_width] for part in range(3))
        q = (q + bias_ref[0:1, :]).astype(half_type).astype(full_type) * HD**-0.5
        index = row + lax.broadcasted_iota(jnp.int32, (BLOCK, LANES), 0)
        segment = jnp.zeros((BLOCK, LANES), jnp.int32)
        end = 0
        for slot in range(slots):
            end = end + len_ref[0, slot]
            segment = segment + jnp.where(index >= end, 1, 0)
        same = spot == segment
        inside = spot <= slots
        q_mark = jnp.where(inside & ~same, -BIG, 0.0)
        k_mark = jnp.where(same, BIG, jnp.where((spot > slots) & (spot <= slots + 3), 1.0, 0.0))
        for head in range(heads):
            pair = slice(head // 2 * LANES, head // 2 * LANES + LANES)
            own = low_half if head % 2 == 0 else ~low_half
            qa_ref[head, rows, :] = jnp.where(own, q[:, pair], q_mark).astype(half_type)
            ka_ref[head, rows, :] = jnp.where(own, k[:, pair], k_mark).astype(half_type)
            va_ref[head, rows, :] = jnp.where(own, v[:, pair], 1.0).astype(half_type)
        return carry

    lax.fori_loop(0, blocks, project, 0)
    pump(0)

    def forward(block, carry):
        spread(1, block, other, other).wait_recv()
        spread(2, block, other, mate).start()
        return carry

    lax.fori_loop(0, count, forward, 0)

    def a1_left(i, carry):
        a1_out(i).wait()
        return carry

    lax.fori_loop(0, blocks, a1_left, 0)
    gbias_ref[...] = jnp.zeros_like(gbias_ref)
    gvec_ref[...] = jnp.zeros_like(gvec_ref)

    share = Share(norm_ref, share_sems)

    def mixed_copy(kind, i, source, target, half_rows):
        rows = pl.ds(pl.multiple_of(i * BLOCK + half_rows * half, half), half)
        return pltpu.make_async_remote_copy(
            src_ref=o_ref.at[rows, :],
            dst_ref=mixed_ref.at[i, :, columns_of(source)],
            send_sem=mixed_sems.at[2 * kind, i],
            recv_sem=mixed_sems.at[2 * kind + 1, i],
            device_id=(me, target),
            device_id_type=MESH,
        )

    peers = ((0, mate, 1 - core), (1, other, core), (2, across, 1 - core))

    def h2_out(i):
        own = pl.ds(pl.multiple_of(i * half, half), half)
        return pltpu.make_async_copy(gh2_ref.at[own, :], h2_hbm.at[own, :], local_sems.at[3, i])

    def attend_block(i):
        rows = pl.ds(pl.multiple_of(i * BLOCK, BLOCK), BLOCK)
        for head in range(heads):
            query = qa_ref[head, rows, :]
            scores = dot(query, ka_ref[head], 1, 1)
            top = jnp.max(scores, axis=1, keepdims=True)
            weights = jnp.exp(scores - top).astype(half_type)
            mixed = dot(weights, va_ref[head])
            turned = pltpu.roll(mixed, HD, 1)
            own = low_half if head % 2 == 0 else ~low_half
            log_total = three_parts(top + jnp.log(jnp.where(own, turned, mixed)))
            marked = query.astype(full_type)
            for part in range(3):
                marked = jnp.where(~own & (spot == slots + 1 + part), -log_total[part], marked)
            qa_ref[head, rows, :] = marked.astype(half_type)
            out = mixed / turned
            if head % 2 == 0:
                before = out
            else:
                pair = slice(head // 2 * LANES, head // 2 * LANES + LANES)
                o_ref[rows, pair] = jnp.where(low_half, before, out).astype(half_type)
        for kind, peer, half_rows in peers[1:] + peers[:1]:
            mixed_copy(kind, i, tensor, peer, half_rows).start()
        here = pl.ds(pl.multiple_of(i * BLOCK + core * half, half), half)
        mixed_ref[i, :, columns_of(tensor)] = o_ref[here, :]

    def norm_block(i):
        own = pl.ds(pl.multiple_of(i * half, half), half)
        for kind, peer, _ in peers:
            mixed_copy(kind, i, peer, peer, 0).wait_recv()
        attn = dot(mixed_ref[i], wo_ref[...], 1, 1)
        hidden = own_ref[own, :].astype(full_type) + attn + vec_ref[0:1, :]
        gh2_ref[own, :] = hidden
        h2_out(i).start()
        unit, _ = normalized(hidden)
        share.put(i, (unit * vec_ref[4:5, :] + vec_ref[5:6, :]).astype(half_type))

    behind = min(2, blocks)

    def attend_step(i, carry):
        attend_block(i)
        for slot in range(1, blocks + 1):

            @pl.when(i == slot - 1)
            def _(slot=slot):
                pump(slot)

        @pl.when(i == behind)
        def _():
            def spread_in(block, carry):
                spread(0, block, mate, mate).wait_recv()
                spread(2, block, across, mate).wait_recv()
                return carry

            lax.fori_loop(0, count, spread_in, 0)

        @pl.when(i >= behind)
        def _():
            norm_block(i - behind)

        return carry

    lax.fori_loop(0, blocks, attend_step, 0)

    def norm_step(i, carry):
        norm_block(i)
        return carry

    lax.fori_loop(blocks - behind, blocks, norm_step, 0)
    pump(blocks + 1)

    whole = [
        pltpu.make_async_copy(source, target, whole_sems.at[k])
        for k, (source, target) in enumerate(
            (
                (own_ref, own_hbm), (qa_ref, qa_hbm), (ka_ref, ka_hbm), (va_ref, va_hbm),
                (o_ref, o_hbm), (w_ref, w_hbm),
            )
        )
    ]
    for copy in whole:
        copy.start()
    down_out = fetch(down_ref, down_hbm, local_sems.at[5])

    def gh2_out(i):
        own = pl.ds(pl.multiple_of(i * half, half), half)
        return pltpu.make_async_copy(gh2_ref.at[own, :], gh2_hbm.at[own, :], local_sems.at[6, i])

    rowsum2 = RowSum(term2, given2, sent2, crossed2, sum2_sems)

    share2 = Share(ga_ref, put_sems)
    ga_out = fetch(ga_ref, ga_hbm, local_sems.at[4])

    def goa_out(i):
        rows = pl.ds(pl.multiple_of(i * BLOCK, BLOCK), BLOCK)
        return pltpu.make_async_copy(
            goa_ref.at[:, rows, :], goa_hbm.at[:, rows, :], local_sems.at[7, i]
        )

    def prepare(i):
        share2.arrived(i)
        ga_out(i).start()
        rows = pl.ds(pl.multiple_of(i * BLOCK, BLOCK), BLOCK)
        go = dot(ga_ref[rows, :], wo_ref[:, columns_of(tensor)]).astype(half_type).astype(full_type)
        both = go * o_ref[rows, :].astype(full_type)
        for head in range(heads):
            pair = slice(head // 2 * LANES, head // 2 * LANES + LANES)
            own = low_half if head % 2 == 0 else ~low_half
            inner = jnp.sum(jnp.where(own, both[:, pair], 0.0), axis=1, keepdims=True)
            filled = jnp.where(own, go[:, pair], 0.0)
            for k, value in enumerate(three_parts(inner)):
                filled = jnp.where(~own & (spot == k), -value, filled)
            goa_ref[head, rows, :] = filled.astype(half_type)
            if head % 2 == 0:
                before = ka_ref[head, rows, :].astype(full_type)
            else:
                k = jnp.where(low_half, before, ka_ref[head, rows, :].astype(full_type))
                kt_ref[pair, rows] = k.T.astype(half_type)
        goa_out(i).start()

    def mlp_block(i):
        rows = pl.ds(pl.multiple_of(i * BLOCK, BLOCK), BLOCK)
        share.arrived(i)
        a2 = norm_ref[rows, :]
        gy = cot_ref[rows, :]
        u, slope = gelu_parts(dot(a2, wd_ref[0]) + b1_ref[...])
        ul = u.astype(half_type)
        gz = (dot(gy, wd_ref[1]) * slope).astype(half_type)
        rowsum2.free(i)
        term2[i % term2.shape[0]] = dot(gz, wd_ref[0], 1, 1).astype(half_type)
        rowsum2.give(i)
        gbias_ref[0:1, :] += jnp.sum(gz.astype(full_type), axis=0, keepdims=True)
        ul_ref[rows, :] = ul
        gz_ref[rows, :] = gz
        down_ref[rows, :] = dot(ul, wd_ref[1], 1, 1).astype(half_type)
        down_out(i).start()
        rowsum2.cross(i)

    chunks = width // BLOCK

    def made_out(kind, c):
        rows = pl.ds(pl.multiple_of(c * BLOCK, BLOCK), BLOCK)
        target = (up_hbm, dn_hbm)[kind].at[rows, :]
        return pltpu.make_async_copy(made.at[kind], target, made_sems.at[kind, c])

    def weight_grads(c):
        columns = pl.ds(pl.multiple_of(c * BLOCK, BLOCK), BLOCK)
        for kind, (left, right) in enumerate(((norm_ref, gz_ref), (cot_ref, ul_ref))):

            @pl.when(c >= 1)
            def _(kind=kind):
                made_out(kind, c - 1).wait()

            made[kind] = dot(left[:, columns], right[...], 0, 0)
            made_out(kind, c).start()

    def back_block(i):
        own = pl.ds(pl.multiple_of(i * half, half), half)
        gn = rowsum2.total(i)
        h2_out(i).wait()
        unit, rate = normalized(gh2_ref[own, :])
        e = gn * vec_ref[4:5, :]
        inner = e - jnp.mean(e, axis=-1, keepdims=True)
        inner = inner - unit * jnp.mean(e * unit, axis=-1, keepdims=True)
        gy = cot_ref[share.rows(i, core), :].astype(full_type)
        gh = gy + rate * inner
        gh2_ref[own, :] = gh
        gh2_out(i).start()
        share2.put(i, gh.astype(half_type))
        gvec_ref[0:1, :] += jnp.sum(gh, axis=0, keepdims=True)
        gvec_ref[1:2, :] += jnp.sum(gy, axis=0, keepdims=True)
        gvec_ref[4:5, :] += jnp.sum(gn * unit, axis=0, keepdims=True)
        gvec_ref[5:6, :] += jnp.sum(gn, axis=0, keepdims=True)

    def mlp_step(i, carry):
        mlp_block(i)
        return carry

    lax.fori_loop(0, blocks, mlp_step, 0)
    late = max(blocks + 2, chunks)

    def tail_step(i, carry):
        @pl.when(i < blocks)
        def _():
            back_block(i)

        @pl.when((i >= 2) & (i < blocks + 2))
        def _():
            prepare(i - 2)

        @pl.when(i < chunks)
        def _():
            weight_grads(i)

        return carry

    lax.fori_loop(0, late, tail_step, 0)
    kt_out = pltpu.make_async_copy(kt_ref, kt_hbm, whole_sems.at[len(whole)])
    kt_out.start()
    for kind in range(2):
        made_out(kind, chunks - 1).wait()

    def copied(i, carry):
        down_out(i).wait()
        gh2_out(i).wait()
        ga_out(i).wait()
        goa_out(i).wait()
        return carry

    lax.fori_loop(0, blocks, copied, 0)
    for copy in whole + [kt_out]:
        copy.wait()
    for piece in attend + dense:
        piece.sent()
    rowsum2.finish()
    share.finish(blocks)
    share2.finish(blocks)

    def spread_out(block, carry):
        spread(0, block, tensor, mate).wait_send()
        spread(1, block, tensor, other).wait_send()
        spread(2, block, other, mate).wait_send()
        return carry

    lax.fori_loop(0, count, spread_out, 0)

    def mixed_out(i, carry):
        for kind, peer, half_rows in peers:
            mixed_copy(kind, i, tensor, peer, half_rows).wait_send()
        return carry

    lax.fori_loop(0, blocks, mixed_out, 0)

    def sent_small(k, carry):
        small_copy(me, (me + k) % count).wait_send()
        return carry

    lax.fori_loop(1, count, sent_small, 0)


class Scatter:
    def __init__(self, view, stage, taken, sems, count):
        self.view, self.stage, self.taken = view, stage, taken
        self.sems, self.count = sems, count
        self.slots = stage.shape[1]
        self.pos = ring_pos(lax.axis_index("dp"), count)
        self.tensor = lax.axis_index("tensor")

    def _copy(self, way, step):
        sign = 1 - 2 * way
        return pltpu.make_async_remote_copy(
            src_ref=self.stage.at[way, step % self.slots],
            dst_ref=self.taken.at[way, step],
            send_sem=self.sems.at[2 * way, step],
            recv_sem=self.sems.at[2 * way + 1, step],
            device_id=(ring_at(self.pos + sign, self.count), self.tensor),
            device_id_type=MESH,
        )

    def begin(self):
        for way in range(2):
            self.stage[way, 0] = self.view(way, 0).astype(half_type)
            self._copy(way, 0).start()

    def advance(self, step):
        for way in range(2):
            self._copy(way, step - 1).wait_recv()
            total = self.taken[way, step - 1].astype(full_type) + self.view(way, step)

            @pl.when(step >= self.slots)
            def _(way=way):
                self._copy(way, step - self.slots).wait_send()

            self.stage[way, step % self.slots] = total.astype(half_type)
            self._copy(way, step).start()

    def total(self, way):
        last = self.count - 2
        self._copy(way, last).wait_recv()
        return self.taken[way, last].astype(full_type) + self.view(way, last + 1)

    def finish(self):
        for step in range(max(self.count - 1 - self.slots, 0), self.count - 1):
            for way in range(2):
                self._copy(way, step).wait_send()


def sent_block(pos, way, step, count):
    return ring_at(pos - (1 - 2 * way) * (1 + step), count)


class Put:
    def __init__(self, held, result, sems):
        self.held, self.result, self.sems = held, result, sems
        self.half = held.shape[0] // sems.shape[1]
        self.dp, tensor = lax.axis_index("dp"), lax.axis_index("tensor")
        self.core = tensor % 2
        self.mate = tensor - tensor % 2 + (tensor + 1) % 2

    def own(self, i):
        return pl.ds(pl.multiple_of(i * self.half, self.half), self.half)

    def _rows(self, i, core):
        return pl.ds(pl.multiple_of((2 * i + core) * self.half, self.half), self.half)

    def _here(self, i):
        target = self.result.at[self._rows(i, self.core), :]
        return pltpu.make_async_copy(self.held.at[self.own(i), :], target, self.sems.at[0, i])

    def _there(self, i, core):
        return pltpu.make_async_remote_copy(
            src_ref=self.held.at[self.own(i), :],
            dst_ref=self.result.at[self._rows(i, core), :],
            send_sem=self.sems.at[1, i],
            recv_sem=self.sems.at[2, i],
            device_id=(self.dp, self.mate),
            device_id_type=MESH,
        )

    def put(self, i, value):
        self.held[self.own(i), :] = value
        self._here(i).start()
        self._there(i, self.core).start()

    def left(self, i):
        self._here(i).wait()
        self._there(i, self.core).wait_send()

    def arrived(self, i):
        self._there(i, 1 - self.core).wait_recv()


def back_kernel(
    count, ga_hbm, o_hbm, qb_hbm, ka_hbm, va_hbm, goa_hbm, kt_hbm, w_hbm, up_hbm, dn_hbm, down_hbm,
    h2_hbm, gh2_hbm, own_hbm, a1_hbm, vec_ref, gbias_ref, gvec_ref,
    layer_hbm, tg_hbm, dense_ref, sum_ref, small_ref,
    ga_ref, o_ref, qb_ref, ka_ref, va_ref, w_ref, wide_ref, gh_ref, own_ref, goa_ref, kt_ref, gqt_ref, gqkv_ref, put_ref,
    given, sent, crossed, term2, given2, sent2, crossed2,
    terms, stage, taken, grads, stage2, taken2, small_mine, small_taken, small_mate,
    sum_sems, sum2_sems, put_sems, put2_sems, scatter_sems, scatter2_sems, small_sems, mate_sems,
    local_sems, terms_sems, whole_sems,
):
    total_rows, width = ga_ref.shape
    local_width = o_ref.shape[1]
    heads = local_width // HD
    blocks = total_rows // BLOCK
    half = BLOCK // 2
    wide = width // count
    hops = count - 1
    lanes = small_ref.shape[1] - local_width
    fold = lanes // wide
    me, tensor = lax.axis_index("dp"), lax.axis_index("tensor")
    mate = tensor - tensor % 2 + (tensor + 1) % 2
    pos = ring_pos(me, count)
    greeted = greet(tensor_peers() + dp_peers(count))

    def own_rows(i):
        return pl.ds(pl.multiple_of(i * half, half), half)

    def place(block):
        return pl.ds(pl.multiple_of(block * wide, wide), wide)

    def own_fetch(source, target, sems):
        return lambda i: pltpu.make_async_copy(
            source.at[own_rows(i), :], target.at[own_rows(i), :], sems.at[i]
        )

    ga_in = fetch(ga_hbm, ga_ref, local_sems.at[0])
    down_in = fetch(down_hbm, wide_ref, local_sems.at[1])
    a1_in = fetch(a1_hbm, wide_ref, local_sems.at[2])
    h2_in = own_fetch(h2_hbm, gh_ref, local_sems.at[3])
    gh2_in = own_fetch(gh2_hbm, gh_ref, local_sems.at[4])
    own_in = own_fetch(own_hbm, own_ref, local_sems.at[5])

    def term_in(way, step):
        rows = place(sent_block(pos, way, step, count))
        source = (up_hbm, dn_hbm)[way].at[rows, :]
        return pltpu.make_async_copy(
            source, terms.at[way, step % 2], terms_sems.at[way, step % 2]
        )

    def each(copy):
        def start(i, carry):
            copy(i).start()
            return carry

        lax.fori_loop(0, blocks, start, 0)

    for step in range(2):
        for way in range(2):
            term_in(way, step).start()
    whole = [
        pltpu.make_async_copy(source, target, whole_sems.at[k])
        for k, (source, target) in enumerate(
            (
                (qb_hbm, qb_ref), (ka_hbm, ka_ref), (va_hbm, va_ref), (goa_hbm, goa_ref),
                (kt_hbm, kt_ref), (o_hbm, o_ref), (w_hbm, w_ref),
            )
        )
    ]
    for copy in whole[:-2]:
        copy.start()
    each(down_in)
    each(h2_in)
    for copy in whole[-2:]:
        copy.start()
    each(ga_in)
    each(own_in)
    small_mine[:, :width] = gvec_ref[...]
    ratio = gbias_ref.shape[1] // local_width
    for r in range(ratio):
        small_mine[1 + r : 2 + r, width:] = gbias_ref[0:1, r * local_width : (r + 1) * local_width]
    small_mine[1 + ratio :, width:] = jnp.zeros((7 - ratio, local_width), full_type)
    greeted()

    pieces = stage.shape[0]
    part = terms.shape[3] // pieces

    def term_view(piece):
        columns = slice(piece * part, (piece + 1) * part)
        return lambda way, step: terms[way, step % 2, :, columns]

    scatters = [
        Scatter(term_view(p), stage.at[p], taken.at[p], scatter_sems.at[p], count)
        for p in range(pieces)
    ]

    def terms_ready(step):
        for way in range(2):
            term_in(way, step).wait()

    def terms_next(step):
        @pl.when(step <= hops)
        def _():
            for way in range(2):
                term_in(way, step).start()

    rowsum = RowSum(wide_ref.reshape(blocks, BLOCK, width), given, sent, crossed, sum_sems)
    layer = Put(put_ref, layer_hbm, put_sems)
    def give_all(i, carry):
        down_in(i).wait()
        rowsum.give(i)
        return carry

    lax.fori_loop(0, blocks, give_all, 0)
    terms_ready(0)
    for scatter in scatters:
        scatter.begin()
    terms_next(2)

    lane = lax.broadcasted_iota(jnp.int32, (BLOCK, LANES), 1)
    low_half = lane < HD
    gqt_ref[...] = jnp.zeros_like(gqt_ref)
    rowsum.cross(0)
    for copy in whole[:-2]:
        copy.wait()

    def output_block(i):
        h2_in(i).wait()
        total = gh_ref[own_rows(i), :] + rowsum.total(i) + vec_ref[1:2, :]
        layer.put(i, total.astype(half_type))
        gh2_in(i).start()

    per = -(-hops // blocks)

    def between(j, piece):
        if piece == 0:

            @pl.when(j >= 1)
            def _():
                output_block(j - 1)

            @pl.when(j < blocks - 1)
            def _():
                rowsum.cross(j + 1)

        for t in range(per):
            hop = j * per + t

            @pl.when((hop >= 1) & (hop < hops))
            def _(hop=hop):
                if piece == 0:
                    terms_ready(hop)
                scatters[piece].advance(hop)
                if piece == pieces - 1:
                    terms_next(hop + 2)

    def keys_block(j, carry):
        rows = pl.ds(pl.multiple_of(j * BLOCK, BLOCK), BLOCK)
        for head in range(heads):
            scores = dot(ka_ref[head, rows, :], qb_ref[head], 1, 1)
            probs = jnp.exp(scores)
            gp = dot(va_ref[head, rows, :], goa_ref[head], 1, 1)
            gs = (probs * gp).astype(half_type)
            gv = dot(probs.astype(half_type), goa_ref[head])
            gk = dot(gs, qb_ref[head])
            own = slice(head * HD, head * HD + HD)
            gqt_ref[own, :] += dot(kt_ref[own, rows], gs)
            if head % 2 == 0:
                gk_even, gv_even = gk, gv
            else:
                for k, value in ((1, (gk_even, gk)), (2, (gv_even, gv))):
                    base = k * local_width + head // 2 * LANES
                    gqkv_ref[rows, base : base + LANES] = jnp.where(low_half, *value).astype(
                        half_type
                    )
            if (head + 1) * pieces % heads == 0:
                between(j, (head + 1) * pieces // heads - 1)
        return carry

    lax.fori_loop(0, blocks, keys_block, 0)

    def turn(i, carry):
        rows = pl.ds(pl.multiple_of(i * BLOCK, BLOCK), BLOCK)
        gqkv_ref[rows, :local_width] = (gqt_ref[:, rows].T * HD**-0.5).astype(half_type)
        return carry

    rowsum2 = RowSum(term2, given2, sent2, crossed2, sum2_sems)

    def norm_term(i):
        rows = pl.ds(pl.multiple_of(i * BLOCK, BLOCK), BLOCK)
        rowsum2.free(i)
        term2[i % term2.shape[0]] = dot(gqkv_ref[rows, :], w_ref[...], 1, 1).astype(half_type)
        rowsum2.give(i)

    lax.fori_loop(0, 2, turn, 0)
    whole[-1].wait()
    norm_term(0)
    norm_term(1)
    rowsum.gone()
    each(a1_in)
    lax.fori_loop(2, blocks, turn, 0)
    rowsum2.cross(0)
    ones = jnp.ones((8, total_rows), half_type)
    bias_query = dot(ones, gqkv_ref[:, :local_width])
    small_mine[0:1, width:] = bias_query[0:1, :]

    def small_copy(kind, source, peer):
        window = pl.ds(pl.multiple_of(peer // fold * lanes, lanes), lanes)
        return pltpu.make_async_remote_copy(
            src_ref=small_mine.at[:, pl.ds(width, local_width) if kind else window],
            dst_ref=small_taken.at[source, :, pl.ds(lanes, local_width) if kind else pl.ds(0, lanes)],
            send_sem=small_sems.at[2 * kind, peer],
            recv_sem=small_sems.at[2 * kind + 1, source],
            device_id=(peer, tensor),
            device_id_type=MESH,
        )

    def send_small(kind):
        def send(k, carry):
            small_copy(kind, me, (me + k) % count).start()
            return carry

        lax.fori_loop(1, count, send, 0)

    send_small(1)

    def arrived_a1(i, carry):
        a1_in(i).wait()
        ga_in(i).wait()
        return carry

    lax.fori_loop(0, blocks, arrived_a1, 0)

    def weight_grads(c, carry):
        columns = pl.ds(pl.multiple_of(c * BLOCK, BLOCK), BLOCK)
        grads[columns, : 3 * local_width] = dot(wide_ref[:, columns], gqkv_ref[...], 0, 0)
        grads[columns, 3 * local_width :] = dot(ga_ref[:, columns], o_ref[...], 0, 0)
        return carry

    chunks = width // BLOCK
    whole[-2].wait()
    lax.fori_loop(0, chunks // 2, weight_grads, 0)
    rowsum2.cross(1)
    output_block(blocks - 1)
    lax.fori_loop(chunks // 2, chunks, weight_grads, 0)
    side = grads.shape[1] // 2

    def grads_view(way, step):
        return grads[
            place(sent_block(pos, way, step, count)), way * side : (way + 1) * side
        ]

    scatter2 = Scatter(grads_view, stage2, taken2, scatter2_sems, count)
    scatter2.begin()

    def layer_left(i, carry):
        layer.left(i)
        layer.arrived(i)
        return carry

    lax.fori_loop(0, blocks, layer_left, 0)
    result = Put(put_ref, tg_hbm, put2_sems)

    def norm_block(i):
        gn = rowsum2.total(i)
        own_in(i).wait()
        gh2_in(i).wait()
        unit, rate = normalized(own_ref[own_rows(i), :].astype(full_type))
        e = gn * vec_ref[2:3, :]
        inner = e - jnp.mean(e, axis=-1, keepdims=True)
        inner = inner - unit * jnp.mean(e * unit, axis=-1, keepdims=True)
        result.put(i, (gh_ref[own_rows(i), :] + rate * inner).astype(half_type))
        small_mine[2:3, :width] += jnp.sum(gn * unit, axis=0, keepdims=True)
        small_mine[3:4, :width] += jnp.sum(gn, axis=0, keepdims=True)

    def end_step(i, carry):
        @pl.when(i < blocks - 2)
        def _():
            norm_term(i + 2)

        norm_block(i)

        @pl.when(i < blocks - 2)
        def _():
            rowsum2.cross(i + 2)

        for t in range(per):
            hop = i * per + t + 1

            @pl.when(hop < hops)
            def _(hop=hop):
                scatter2.advance(hop)

        return carry

    lax.fori_loop(0, blocks, end_step, 0)
    send_small(0)
    terms_ready(hops)
    for way in range(2):
        for p, scatter in enumerate(scatters):
            dense_ref[way, :, p * part : (p + 1) * part] = scatter.total(way)
        total = scatter2.total(way)
        for k in range(2):
            sum_ref[2 * way + k] = total[:, k * local_width : (k + 1) * local_width]
    for kind in range(2):
        window = pl.ds(pl.multiple_of(me // fold * lanes, lanes), lanes)
        here = slice(lanes, lanes + local_width) if kind else slice(0, lanes)
        small_taken[me, :, here] = small_mine[:, width:] if kind else small_mine[:, window]

        def take(k, carry, kind=kind):
            source = (me + k) % count
            small_copy(kind, source, source).wait_recv()
            return carry

        lax.fori_loop(1, count, take, 0)
    total = small_taken[0]
    for j in range(1, count):
        total = total + small_taken[j]
    small_ref[...] = total
    pair = pltpu.make_async_remote_copy(
        src_ref=small_ref.at[:, pl.ds(0, lanes)],
        dst_ref=small_mate,
        send_sem=mate_sems.at[0],
        recv_sem=mate_sems.at[1],
        device_id=(me, mate),
        device_id_type=MESH,
    )
    pair.start()
    pair.wait()
    small_ref[:, :lanes] = total[:, :lanes] + small_mate[...]

    def result_left(i, carry):
        result.left(i)
        result.arrived(i)
        return carry

    lax.fori_loop(0, blocks, result_left, 0)
    for scatter in scatters + [scatter2]:
        scatter.finish()
    rowsum.finish(given=False)
    rowsum2.finish()
    for kind in range(2):

        def done(k, carry, kind=kind):
            small_copy(kind, me, (me + k) % count).wait_send()
            return carry

        lax.fori_loop(1, count, done, 0)


def permuted(x, owner, back):
    rows, width = x.shape
    count = owner.shape[0]
    order = jnp.argsort(owner) if back else owner
    return jnp.take(x.reshape(rows, count, -1), order, axis=1).reshape(rows, width)


def adamw_step(weight, first, second, grad, rate, decay):
    first_next = first_decay * first + (1.0 - first_decay) * grad
    second_next = second_decay * second + (1.0 - second_decay) * grad * grad
    first_hat = first_next / (1.0 - first_decay**STEP)
    second_hat = second_next / (1.0 - second_decay**STEP)
    update = first_hat / (jnp.sqrt(second_hat) + adam_epsilon) + decay * weight
    return (first_next, second_next, weight - rate * update)


def last_kernel(rates, owner_ref, *refs):
    count = owner_ref.shape[0]
    given, refs = refs[:5], refs[5:]
    layer, grad, weight_sum, dense_sum, small = given
    state, refs = refs[:15], refs[15:]
    results, outs = refs[:2], refs[2:]

    def step(k, grad, at=(Ellipsis,)):
        new = adamw_step(*(ref[at] for ref in state[3 * k : 3 * k + 3]), grad, *rates[k])
        for ref, value in zip(outs[3 * k : 3 * k + 3], new):
            ref[at] = value

    wide = layer.shape[1] // count
    if wide % LANES == 0:
        for j in range(count):
            natural = pl.ds(pl.multiple_of(owner_ref[j] * wide, wide), wide)
            for x, y in zip((layer, grad), results):
                y[:, natural] = x[:, j * wide : (j + 1) * wide]
    else:
        for x, y in zip((layer, grad), results):
            y[...] = x[...]
    step(0, weight_sum[0:3])
    step(1, weight_sum[3])
    ratio, local_width = state[6].shape[2:]
    for r in range(ratio):
        step(
            2,
            dense_sum[:, :, r * local_width : (r + 1) * local_width],
            (slice(None), slice(None), r, slice(None)),
        )
    me = lax.axis_index("dp")
    lanes = small.shape[1] - local_width

    def chosen(x, start, size):
        row = lax.broadcasted_iota(jnp.int32, (x.shape[1], size), 0)
        column = lax.broadcasted_iota(jnp.int32, (x.shape[1], size), 1)
        pick = jnp.where(row == column + start, 1.0, 0.0).astype(half_type)
        return sum(dot(part.astype(half_type), pick) for part in three_parts(x))

    narrow, wide = state[9].shape[1], state[12].shape[1]
    step(3, chosen(small[:, lanes:], owner_ref[me] * narrow, narrow)[: 1 + ratio])
    step(4, chosen(small[:, :lanes], me % (lanes // wide) * wide, wide)[:6])


def last(owner, layer_output, tokens_grad, weight_sum, dense_sum, small_sum, *state):
    steps = 4 if dense_sum.shape[1] % 128 == 0 else 1
    rates = (
        (matrix_rate, matrix_decay),
        (output_rate, matrix_decay),
        (matrix_rate, matrix_decay),
        (bias_rate, 0.0),
        (vector_rate, 0.0),
    )

    def spec(x, dim):
        shape = tuple(n // steps if k == dim else n for k, n in enumerate(x.shape))
        return pl.BlockSpec(shape, lambda i, *_: tuple(i if k == dim else 0 for k in range(x.ndim)))

    dims = [0, 0, 1, 1, None] + [1] * 3 + [0] * 3 + [1] * 3 + [None] * 6
    operands = (layer_output, tokens_grad, weight_sum, dense_sum, small_sum) + state
    specs = [spec(x, dim) for x, dim in zip(operands, dims)]
    outs = operands[:2] + state
    return pl.pallas_call(
        functools.partial(last_kernel, rates),
        out_shape=[jax.ShapeDtypeStruct(x.shape, x.dtype) for x in outs],
        grid_spec=pltpu.PrefetchScalarGridSpec(
            num_scalar_prefetch=1, grid=(steps,), in_specs=specs, out_specs=specs[:2] + specs[5:]
        ),
        compiler_params=pltpu.CompilerParams(vmem_limit_bytes=60 * 2**20),
    )(owner, *operands)


def call(kernel, collective, outs, scratch, operands, spaces, limit=62):
    spec = {
        "s": pl.BlockSpec(memory_space=pltpu.SMEM),
        "v": pl.BlockSpec(memory_space=pltpu.VMEM),
        "h": pl.BlockSpec(memory_space=pl.ANY),
    }
    return pl.pallas_call(
        kernel,
        out_shape=[jax.ShapeDtypeStruct(shape, dtype) for shape, dtype in outs],
        in_specs=[spec[c] for c in spaces[0]],
        out_specs=[spec[c] for c in spaces[1]],
        scratch_shapes=scratch,
        compiler_params=pltpu.CompilerParams(
            collective_id=collective, has_side_effects=True, vmem_limit_bytes=limit * 2**20
        ),
    )(*operands)


def dma(*shape):
    return pltpu.SemaphoreType.DMA(shape)


def local(
    tokens,
    lengths,
    owner,
    attend_master,
    attend_first,
    attend_second,
    output_master,
    output_first,
    output_second,
    dense_master,
    dense_first,
    dense_second,
    bias_master,
    bias_first,
    bias_second,
    vector_master,
    vector_first,
    vector_second,
    cotangent,
):
    count = owner.shape[0]
    rows, width = tokens.shape
    local_width = output_master.shape[1]
    ratio = dense_master.shape[2]
    hidden = ratio * local_width
    heads = local_width // HD
    blocks = rows // BLOCK
    half = BLOCK // 2
    wide = width // count
    lanes = max(LANES, wide)
    tok, cot = tokens, cotangent
    if wide % LANES:
        tok, cot = (permuted(x, owner, False) for x in (tokens, cotangent))
    row_sum = [pltpu.VMEM((blocks, half, width), half_type)] * 3
    two_terms = pltpu.VMEM((2, BLOCK, width), half_type)
    heads_shape = (heads, rows, LANES)
    small = (8, lanes + local_width)
    a1, ga, h2, own, qb, ka, va, o, w, gh2, down, up, dn, goa, kt, vec, gbias, gvec = call(
        functools.partial(front_kernel, count),
        0,
        [
            ((rows, width), half_type),
            ((rows, width), half_type),
            ((rows // 2, width), full_type),
            ((rows // 2, width), half_type),
            (heads_shape, half_type),
            (heads_shape, half_type),
            (heads_shape, half_type),
            ((rows, local_width), half_type),
            ((width, 3 * local_width), half_type),
            ((rows // 2, width), full_type),
            ((rows, width), half_type),
            ((width, hidden), full_type),
            ((width, hidden), full_type),
            (heads_shape, half_type),
            ((local_width, rows), half_type),
            ((8, width), full_type),
            ((8, hidden), full_type),
            ((8, width), full_type),
        ],
        [
            pltpu.VMEM((rows // 2, width), half_type),
            *[pltpu.VMEM(heads_shape, half_type)] * 3,
            pltpu.VMEM((rows, local_width), half_type),
            pltpu.VMEM((width, 3 * local_width), half_type),
            pltpu.VMEM((width, width), half_type),
            pltpu.VMEM((rows // 2, width), full_type),
            pltpu.VMEM((rows, width), half_type),
            *[pltpu.VMEM((rows, hidden), half_type)] * 2,
            pltpu.VMEM((2, BLOCK, hidden), full_type),
            *[pltpu.VMEM((rows, width), half_type)] * 2,
            pltpu.VMEM((2, width, hidden), half_type),
            pltpu.VMEM((rows, width), half_type),
            pltpu.VMEM(heads_shape, half_type),
            pltpu.VMEM((local_width, rows), half_type),
            pltpu.VMEM((8, local_width), full_type),
            pltpu.VMEM((1, hidden), full_type),
            pltpu.VMEM(small, full_type),
            pltpu.VMEM((count,) + small, full_type),
            pltpu.VMEM((blocks, half, width), half_type),
            two_terms,
            *row_sum,
            dma(6, 4, count // 2),
            dma(2, count),
            dma(6, count),
            dma(6, blocks),
            dma(4, blocks),
            dma(2, blocks),
            dma(2, blocks),
            dma(8, blocks),
            dma(7),
            dma(2, width // BLOCK),
        ],
        (
            lengths, owner, tok, cot, attend_master, output_master, dense_master, vector_master,
            bias_master,
        ),
        ("sshhvvvvv", "h" * 15 + "vvv"),
    )
    pieces = 2
    row_blocks = pltpu.VMEM((blocks, half, width), half_type)
    row_slots = pltpu.VMEM((min(3, blocks), half, width), half_type)
    part, side = hidden // pieces, 2 * local_width
    layer_output, tokens_grad, dense_sum, weight_sum, small_sum = call(
        functools.partial(back_kernel, count),
        1,
        [
            ((rows, width), half_type),
            ((rows, width), half_type),
            ((2, wide, hidden), full_type),
            ((4, wide, local_width), full_type),
            ((8, lanes + local_width), full_type),
        ],
        [
            pltpu.VMEM((rows, width), half_type),
            pltpu.VMEM((rows, local_width), half_type),
            *[pltpu.VMEM(heads_shape, half_type)] * 3,
            pltpu.VMEM((width, 3 * local_width), half_type),
            pltpu.VMEM((rows, width), half_type),
            pltpu.VMEM((rows // 2, width), full_type),
            pltpu.VMEM((rows // 2, width), half_type),
            pltpu.VMEM(heads_shape, half_type),
            pltpu.VMEM((local_width, rows), half_type),
            pltpu.VMEM((local_width, rows), full_type),
            pltpu.VMEM((rows, 3 * local_width), half_type),
            pltpu.VMEM((rows // 2, width), half_type),
            row_blocks,
            row_slots,
            row_blocks,
            two_terms,
            row_blocks,
            row_slots,
            row_blocks,
            pltpu.VMEM((2, 2, wide, hidden), full_type),
            pltpu.VMEM((pieces, 2, 2, wide, part), half_type),
            pltpu.VMEM((pieces, 2, count - 1, wide, part), half_type),
            pltpu.VMEM((width, 4 * local_width), full_type),
            pltpu.VMEM((2, 2, wide, side), half_type),
            pltpu.VMEM((2, count - 1, wide, side), half_type),
            pltpu.VMEM((8, width + local_width), full_type),
            pltpu.VMEM((count, 8, lanes + local_width), full_type),
            pltpu.VMEM((8, lanes), full_type),
            dma(4, blocks),
            dma(4, blocks),
            dma(3, blocks),
            dma(3, blocks),
            dma(pieces, 4, count - 1),
            dma(4, count - 1),
            dma(4, count),
            dma(2),
            dma(6, blocks),
            dma(2, 2),
            dma(7),
        ],
        (ga, o, qb, ka, va, goa, kt, w, up, dn, down, h2, gh2, own, a1, vec, gbias, gvec),
        ("h" * 15 + "vvv", "hhvvv"),
    )
    if wide % LANES:
        layer_output, tokens_grad = (permuted(x, owner, True) for x in (layer_output, tokens_grad))
    return tuple(
        last(
            owner, layer_output, tokens_grad, weight_sum, dense_sum, small_sum,
            attend_master, attend_first, attend_second,
            output_master, output_first, output_second,
            dense_master, dense_first, dense_second,
            bias_master, bias_first, bias_second,
            vector_master, vector_first, vector_second,
        )
    )


def solution(mesh):
    return jax.shard_map(
        local,
        mesh=mesh,
        in_specs=(
            P("dp", None),
            P("dp", None),
            P(),
            P(None, "dp", "tensor"),
            P(None, "dp", "tensor"),
            P(None, "dp", "tensor"),
            P("dp", "tensor"),
            P("dp", "tensor"),
            P("dp", "tensor"),
            P(None, "dp", None, "tensor"),
            P(None, "dp", None, "tensor"),
            P(None, "dp", None, "tensor"),
            P(None, ("tensor", "dp")),
            P(None, ("tensor", "dp")),
            P(None, ("tensor", "dp")),
            P(None, "dp"),
            P(None, "dp"),
            P(None, "dp"),
            P("dp", None),
        ),
        out_specs=(
            P("dp", None),
            P("dp", None),
            P(None, "dp", "tensor"),
            P(None, "dp", "tensor"),
            P(None, "dp", "tensor"),
            P("dp", "tensor"),
            P("dp", "tensor"),
            P("dp", "tensor"),
            P(None, "dp", None, "tensor"),
            P(None, "dp", None, "tensor"),
            P(None, "dp", None, "tensor"),
            P(None, ("tensor", "dp")),
            P(None, ("tensor", "dp")),
            P(None, ("tensor", "dp")),
            P(None, "dp"),
            P(None, "dp"),
            P(None, "dp"),
        ),
        check_vma=False,
    )
```

profile of v0, /device:TPU:0, one launch (start us, length us, event | category | flops | bytes accessed | tf_op | source)
XLA Modules:
  0.0 240.1 jit_solution(6115521934435441240)
XLA Ops:
  0.7 128.2 %shard_map.314 = (bf16[1792,1024]{1,0:T(8,128)(2,1)}, bf16[1792,1024]{1,0:T(8,128)(2,1)}, f32[896,1024]{1,0:T(8,128)}, bf16[896,1024]{1,0:T(8,128)(2,1)}, bf16[4...) custom-call(s32[1,8]{1,0:T(1,128)} %len_ref.1, ...), custom_call_target="tpu_custom_call" | custom-call | tf_op jit(solution)/shard_map/pallas_call | solution.py:1290
  128.9 98.3 %shard_map.315 = (bf16[1792,1024]{1,0:T(8,128)(2,1)}, bf16[1792,1024]{1,0:T(8,128)(2,1)}, f32[2,128,1024]{2,1,0:T(8,128)}, f32[4,128,256]{2,1,0:T(8,128)}, f32[8,384]{1,0:T(8,128)}) custom-call(bf16[1792,1024]{1,0:T(8,128)(2,1)} %get-tuple-element.40.ga_hbm, bf16[1792,256]{1,0:T(8,128)(2,1)} %get-tuple-element.41.o_hbm, ...), custom_call_target="tpu_custom_call" | custom-call | tf_op jit(solution)/shard_map/pallas_call | solution.py:1290
  227.2 12.7 %shard_map.316 = (bf16[1792,1024]{1,0:T(8,128)(2,1)}, bf16[1792,1024]{1,0:T(8,128)(2,1)}, f32[3,128,256]{2,1,0:T(8,128)}, f32[3,128,256]{2,1,0:T(8,128)}, f32[3,...) custom-call(s32[8]{0:T(128)} %owner_ref.3, ...), custom_call_target="tpu_custom_call" | custom-call | tf_op jit(solution)/shard_map/pallas_call | solution.py:1274
where the time goes:
time: 240 us
  Pallas kernels  239 us (100%)
    pallas_call x2, Pallas kernels, call(): pl.pallas_call(kernel, out_shape=[jax.ShapeDtypeStruct(shape, dtype) for...  226 us
    pallas_call x1, Pallas kernels, last(): pl.pallas_call(functools.partial(last_kernel, rates), out_shape=[jax.Shap...  12.7 us

commit v1 on v0

--- a/solution.py
+++ b/solution.py
@@ -91,10 +91,10 @@
 
 
 class RowSum:
-    def __init__(self, term, given, sent, crossed, sems):
+    def __init__(self, term, given, sent, crossed, sems, first=0):
         self.term, self.given, self.sent_ref, self.crossed = term, given, sent, crossed
         self.slots, self.sent_slots, self.blocks = term.shape[0], sent.shape[0], given.shape[0]
-        self.sems = sems
+        self.sems, self.first = sems, first
         self.half = given.shape[1]
         self.dp, tensor = lax.axis_index("dp"), lax.axis_index("tensor")
         self.core = tensor % 2
@@ -139,7 +139,7 @@
         mine = self.term[i % self.slots, self.rows(self.core), :].astype(full_type)
         if self.sent_slots < self.blocks:
 
-            @pl.when(i >= self.sent_slots)
+            @pl.when(i >= self.sent_slots + self.first)
             def _():
                 self._cross(i - self.sent_slots).wait_send()
 
@@ -148,16 +148,26 @@
         self._cross(i).start()
 
     def total(self, i):
-        self._cross(i).wait_recv()
+        if self.first:
+
+            @pl.when(i >= self.first)
+            def _():
+                self._cross(i).wait_recv()
+
+        else:
+            self._cross(i).wait_recv()
         mine = self.sent_ref[i % self.sent_slots].astype(full_type)
         return mine + self.crossed[i].astype(full_type)
+
+    def ready(self, i):
+        self._cross(i).wait_recv()
 
     def gone(self):
         def given(i, carry):
             self._give(i).wait_send()
             return carry
 
-        lax.fori_loop(max(self.blocks - self.slots, 0), self.blocks, given, 0)
+        lax.fori_loop(max(self.blocks - self.slots, self.first), self.blocks, given, 0)
 
     def finish(self, given=True):
         if given:
@@ -167,7 +177,7 @@
             self._cross(i).wait_send()
             return carry
 
-        lax.fori_loop(max(self.blocks - self.sent_slots, 0), self.blocks, crossed, 0)
+        lax.fori_loop(max(self.blocks - self.sent_slots, self.first), self.blocks, crossed, 0)
 
 
 class Share:
@@ -268,12 +278,12 @@
 def front_kernel(
     count, len_ref, owner_ref, tok_hbm, cot_hbm, att_ref, out_ref, dense_ref, vector_ref, split_ref,
     a1_hbm, ga_hbm, h2_hbm, own_hbm, qa_hbm, ka_hbm, va_hbm, o_hbm, w_hbm, gh2_hbm, down_hbm,
-    up_hbm, dn_hbm, goa_hbm, kt_hbm, vec_ref, gbias_ref, gvec_ref,
+    up_hbm, dn_hbm, goa_hbm, kt_hbm, first_hbm, vec_ref, gbias_ref, gvec_ref,
     own_ref, qa_ref, ka_ref, va_ref, o_ref, w_ref, wo_ref, gh2_ref, down_ref, ul_ref, gz_ref, made,
     norm_ref, cot_ref, wd_ref, ga_ref, goa_ref, kt_ref, bias_ref, b1_ref, small_ref, smalls,
-    mixed_ref, term2, given2, sent2, crossed2,
+    mixed_ref, term2, given2, sent2, crossed2, given3, sent3, crossed3,
     gather_sems, small_sems, spread_sems, mixed_sems, sum2_sems, share_sems, put_sems, local_sems,
-    whole_sems, made_sems,
+    whole_sems, made_sems, sum3_sems,
 ):
     me, tensor = lax.axis_index("dp"), lax.axis_index("tensor")
     total_rows, width = norm_ref.shape
@@ -434,7 +444,7 @@
         if step == steps - 1:
             for piece in dense:
                 piece.advance(0)
-        upto = min(blocks, -(-blocks * step // (steps - 1)))
+        upto = min(blocks, -(-blocks * step // steps))
         if upto > done:
             lax.fori_loop(done, upto, norm_rows, 0)
         done = max(done, upto)
@@ -443,7 +453,7 @@
 
     def pump(slot):
         for k, (piece, step) in enumerate(pumps):
-            if min(blocks + 1, (13 * k + 2) // 10 * 8 // len(pumps)) == slot:
+            if min(blocks + 1, (14 * k + 9) // 10 * 8 // len(pumps)) == slot:
                 piece.advance(step)
 
     lane = lax.broadcasted_iota(jnp.int32, (BLOCK, LANES), 1)
@@ -691,6 +701,11 @@
         return carry
 
     lax.fori_loop(0, blocks, mlp_step, 0)
+    rowsum3 = RowSum(
+        down_ref.reshape(blocks, BLOCK, width), given3, sent3, crossed3, sum3_sems
+    )
+    rowsum3.give(0)
+
     late = max(blocks + 2, chunks)
 
     def tail_step(i, carry):
@@ -705,6 +720,10 @@
         @pl.when(i < chunks)
         def _():
             weight_grads(i)
+
+        @pl.when(i == 0)
+        def _():
+            rowsum3.cross(0)
 
         return carry
 
@@ -713,6 +732,13 @@
     kt_out.start()
     for kind in range(2):
         made_out(kind, chunks - 1).wait()
+    rowsum3.ready(0)
+    first_out = [
+        pltpu.make_async_copy(ref.at[0], first_hbm.at[k], whole_sems.at[len(whole) + 1 + k])
+        for k, ref in enumerate((sent3, crossed3))
+    ]
+    for copy in first_out:
+        copy.start()
 
     def copied(i, carry):
         down_out(i).wait()
@@ -722,11 +748,12 @@
         return carry
 
     lax.fori_loop(0, blocks, copied, 0)
-    for copy in whole + [kt_out]:
+    for copy in whole + [kt_out] + first_out:
         copy.wait()
     for piece in attend + dense:
         piece.sent()
     rowsum2.finish()
+    rowsum3.finish()
     share.finish(blocks)
     share2.finish(blocks)
 
@@ -846,7 +873,7 @@
 
 def back_kernel(
     count, ga_hbm, o_hbm, qb_hbm, ka_hbm, va_hbm, goa_hbm, kt_hbm, w_hbm, up_hbm, dn_hbm, down_hbm,
-    h2_hbm, gh2_hbm, own_hbm, a1_hbm, vec_ref, gbias_ref, gvec_ref,
+    h2_hbm, gh2_hbm, own_hbm, a1_hbm, first_hbm, vec_ref, gbias_ref, gvec_ref,
     layer_hbm, tg_hbm, dense_ref, sum_ref, small_ref,
     ga_ref, o_ref, qb_ref, ka_ref, va_ref, w_ref, wide_ref, gh_ref, own_ref, goa_ref, kt_ref, gqt_ref, gqkv_ref, put_ref,
     given, sent, crossed, term2, given2, sent2, crossed2,
@@ -908,13 +935,16 @@
         for k, (source, target) in enumerate(
             (
                 (qb_hbm, qb_ref), (ka_hbm, ka_ref), (va_hbm, va_ref), (goa_hbm, goa_ref),
-                (kt_hbm, kt_ref), (o_hbm, o_ref), (w_hbm, w_ref),
+                (kt_hbm, kt_ref), (first_hbm.at[0], sent.at[0]), (first_hbm.at[1], crossed.at[0]),
+                (o_hbm, o_ref), (w_hbm, w_ref),
             )
         )
     ]
-    for copy in whole[:-2]:
+    for copy in whole[:-4]:
         copy.start()
     each(down_in)
+    for copy in whole[-4:-2]:
+        copy.start()
     each(h2_in)
     for copy in whole[-2:]:
         copy.start()
@@ -949,14 +979,8 @@
             for way in range(2):
                 term_in(way, step).start()
 
-    rowsum = RowSum(wide_ref.reshape(blocks, BLOCK, width), given, sent, crossed, sum_sems)
+    rowsum = RowSum(wide_ref.reshape(blocks, BLOCK, width), given, sent, crossed, sum_sems, 1)
     layer = Put(put_ref, layer_hbm, put_sems)
-    def give_all(i, carry):
-        down_in(i).wait()
-        rowsum.give(i)
-        return carry
-
-    lax.fori_loop(0, blocks, give_all, 0)
     terms_ready(0)
     for scatter in scatters:
         scatter.begin()
@@ -965,7 +989,10 @@
     lane = lax.broadcasted_iota(jnp.int32, (BLOCK, LANES), 1)
     low_half = lane < HD
     gqt_ref[...] = jnp.zeros_like(gqt_ref)
-    rowsum.cross(0)
+    down_in(0).wait()
+    for i in range(1, 3):
+        down_in(i).wait()
+        rowsum.give(i)
     for copy in whole[:-2]:
         copy.wait()
 
@@ -983,6 +1010,11 @@
             @pl.when(j >= 1)
             def _():
                 output_block(j - 1)
+
+            @pl.when(j < blocks - 3)
+            def _():
+                down_in(j + 3).wait()
+                rowsum.give(j + 3)
 
             @pl.when(j < blocks - 1)
             def _():
@@ -1037,14 +1069,15 @@
         term2[i % term2.shape[0]] = dot(gqkv_ref[rows, :], w_ref[...], 1, 1).astype(half_type)
         rowsum2.give(i)
 
-    lax.fori_loop(0, 2, turn, 0)
+    turn(0, 0)
     whole[-1].wait()
     norm_term(0)
-    norm_term(1)
     rowsum.gone()
     each(a1_in)
+    turn(1, 0)
+    norm_term(1)
+    rowsum2.cross(0)
     lax.fori_loop(2, blocks, turn, 0)
-    rowsum2.cross(0)
     ones = jnp.ones((8, total_rows), half_type)
     bias_query = dot(ones, gqkv_ref[:, :local_width])
     small_mine[0:1, width:] = bias_query[0:1, :]
@@ -1084,10 +1117,8 @@
 
     chunks = width // BLOCK
     whole[-2].wait()
-    lax.fori_loop(0, chunks // 2, weight_grads, 0)
     rowsum2.cross(1)
-    output_block(blocks - 1)
-    lax.fori_loop(chunks // 2, chunks, weight_grads, 0)
+    lax.fori_loop(0, chunks, weight_grads, 0)
     side = grads.shape[1] // 2
 
     def grads_view(way, step):
@@ -1097,6 +1128,7 @@
 
     scatter2 = Scatter(grads_view, stage2, taken2, scatter2_sems, count)
     scatter2.begin()
+    output_block(blocks - 1)
 
     def layer_left(i, carry):
         layer.left(i)
@@ -1341,7 +1373,7 @@
     two_terms = pltpu.VMEM((2, BLOCK, width), half_type)
     heads_shape = (heads, rows, LANES)
     small = (8, lanes + local_width)
-    a1, ga, h2, own, qb, ka, va, o, w, gh2, down, up, dn, goa, kt, vec, gbias, gvec = call(
+    a1, ga, h2, own, qb, ka, va, o, w, gh2, down, up, dn, goa, kt, first, vec, gbias, gvec = call(
         functools.partial(front_kernel, count),
         0,
         [
@@ -1360,6 +1392,7 @@
             ((width, hidden), full_type),
             (heads_shape, half_type),
             ((local_width, rows), half_type),
+            ((2, half, width), half_type),
             ((8, width), full_type),
             ((8, hidden), full_type),
             ((8, width), full_type),
@@ -1386,6 +1419,7 @@
             pltpu.VMEM((blocks, half, width), half_type),
             two_terms,
             *row_sum,
+            *[pltpu.VMEM((1, half, width), half_type)] * 3,
             dma(6, 4, count // 2),
             dma(2, count),
             dma(6, count),
@@ -1394,14 +1428,15 @@
             dma(2, blocks),
             dma(2, blocks),
             dma(8, blocks),
-            dma(7),
+            dma(9),
             dma(2, width // BLOCK),
+            dma(4, 1),
         ],
         (
             lengths, owner, tok, cot, attend_master, output_master, dense_master, vector_master,
             bias_master,
         ),
-        ("sshhvvvvv", "h" * 15 + "vvv"),
+        ("sshhvvvvv", "h" * 16 + "vvv"),
     )
     pieces = 2
     row_blocks = pltpu.VMEM((blocks, half, width), half_type)
@@ -1456,10 +1491,13 @@
             dma(2),
             dma(6, blocks),
             dma(2, 2),
-            dma(7),
+            dma(9),
         ],
-        (ga, o, qb, ka, va, goa, kt, w, up, dn, down, h2, gh2, own, a1, vec, gbias, gvec),
-        ("h" * 15 + "vvv", "hhvvv"),
+        (
+            ga, o, qb, ka, va, goa, kt, w, up, dn, down, h2, gh2, own, a1, first, vec, gbias,
+            gvec,
+        ),
+        ("h" * 16 + "vvv", "hhvvv"),
     )
     if wide % LANES:
         layer_output, tokens_grad = (permuted(x, owner, True) for x in (layer_output, tokens_grad))

time: 240 us -> 236 us (0.983)
  Pallas kernels: 239 us -> 235 us
    pallas_call x2, Pallas kernels: 226 us -> 222 us  [call(): pl.pallas_call(kernel, out_shape=[jax.ShapeDtypeStruct(shape, dtype) for...]
where the time goes in v1:
time: 236 us
  Pallas kernels  235 us (100%)
    pallas_call x2, Pallas kernels, call(): pl.pallas_call(kernel, out_shape=[jax.ShapeDtypeStruct(shape, dtype) for...  222 us
    pallas_call x1, Pallas kernels, last(): pl.pallas_call(functools.partial(last_kernel, rates), out_shape=[jax.Shap...  12.7 us

profile of v1, /device:TPU:0, one launch (start us, length us, event | category | flops | bytes accessed | tf_op | source)
XLA Modules:
  0.0 235.9 jit_solution(18365522291837856879)
XLA Ops:
  0.7 125.8 %shard_map.314 = (bf16[1792,1024]{1,0:T(8,128)(2,1)}, bf16[1792,1024]{1,0:T(8,128)(2,1)}, f32[896,1024]{1,0:T(8,128)}, bf16[896,1024]{1,0:T(8,128)(2,1)}, bf16[4...) custom-call(s32[1,8]{1,0:T(1,128)} %len_ref.1, ...), custom_call_target="tpu_custom_call" | custom-call | tf_op jit(solution)/shard_map/pallas_call | solution.py:1322
  126.5 96.5 %shard_map.315 = (bf16[1792,1024]{1,0:T(8,128)(2,1)}, bf16[1792,1024]{1,0:T(8,128)(2,1)}, f32[2,128,1024]{2,1,0:T(8,128)}, f32[4,128,256]{2,1,0:T(8,128)}, f32[8,384]{1,0:T(8,128)}) custom-call(bf16[1792,1024]{1,0:T(8,128)(2,1)} %get-tuple-element.41.ga_hbm, bf16[1792,256]{1,0:T(8,128)(2,1)} %get-tuple-element.42.o_hbm, ...), custom_call_target="tpu_custom_call" | custom-call | tf_op jit(solution)/shard_map/pallas_call | solution.py:1322
  222.9 12.7 %shard_map.316 = (bf16[1792,1024]{1,0:T(8,128)(2,1)}, bf16[1792,1024]{1,0:T(8,128)(2,1)}, f32[3,128,256]{2,1,0:T(8,128)}, f32[3,128,256]{2,1,0:T(8,128)}, f32[3,...) custom-call(s32[8]{0:T(128)} %owner_ref.3, ...), custom_call_target="tpu_custom_call" | custom-call | tf_op jit(solution)/shard_map/pallas_call | solution.py:1306

commit v2 on v1

--- a/solution.py
+++ b/solution.py
@@ -1175,7 +1175,11 @@
     terms_ready(hops)
     for way in range(2):
         for p, scatter in enumerate(scatters):
-            dense_ref[way, :, p * part : (p + 1) * part] = scatter.total(way)
+            total = scatter.total(way)
+            for r in range(part // local_width):
+                dense_ref[way, :, p * part // local_width + r, :] = total[
+                    :, r * local_width : (r + 1) * local_width
+                ]
         total = scatter2.total(way)
         for k in range(2):
             sum_ref[2 * way + k] = total[:, k * local_width : (k + 1) * local_width]
@@ -1264,13 +1268,8 @@
             y[...] = x[...]
     step(0, weight_sum[0:3])
     step(1, weight_sum[3])
+    step(2, dense_sum[...])
     ratio, local_width = state[6].shape[2:]
-    for r in range(ratio):
-        step(
-            2,
-            dense_sum[:, :, r * local_width : (r + 1) * local_width],
-            (slice(None), slice(None), r, slice(None)),
-        )
     me = lax.axis_index("dp")
     lanes = small.shape[1] - local_width
 
@@ -1448,7 +1447,7 @@
         [
             ((rows, width), half_type),
             ((rows, width), half_type),
-            ((2, wide, hidden), full_type),
+            (dense_master.shape, full_type),
             ((4, wide, local_width), full_type),
             ((8, lanes + local_width), full_type),
         ],

time: 236 us -> 235 us (level)
  no operation moved by 1% of the time
where the time goes in v2:
time: 235 us; the launch traced here: 234 us
  Pallas kernels  233 us (99%)
    pallas_call x2, Pallas kernels, call(): pl.pallas_call(kernel, out_shape=[jax.ShapeDtypeStruct(shape, dtype) for...  222 us
    pallas_call x1, Pallas kernels, last(): pl.pallas_call(functools.partial(last_kernel, rates), out_shape=[jax.Shap...  11.2 us

profile of v2, /device:TPU:0, one launch (start us, length us, event | category | flops | bytes accessed | tf_op | source)
XLA Modules:
  0.0 234.3 jit_solution(7782918276600791606)
XLA Ops:
  0.7 125.8 %shard_map.314 = (bf16[1792,1024]{1,0:T(8,128)(2,1)}, bf16[1792,1024]{1,0:T(8,128)(2,1)}, f32[896,1024]{1,0:T(8,128)}, bf16[896,1024]{1,0:T(8,128)(2,1)}, bf16[4...) custom-call(s32[1,8]{1,0:T(1,128)} %len_ref.1, ...), custom_call_target="tpu_custom_call" | custom-call | tf_op jit(solution)/shard_map/pallas_call | solution.py:1321
  126.5 96.5 %shard_map.315 = (bf16[1792,1024]{1,0:T(8,128)(2,1)}, bf16[1792,1024]{1,0:T(8,128)(2,1)}, f32[2,128,4,256]{3,2,1,0:T(4,128)}, f32[4,128,256]{2,1,0:T(8,128)}, f32[8,384]{1,0:T(8,128)}) custom-call(bf16[1792,1024]{1,0:T(8,128)(2,1)} %get-tuple-element.41.ga_hbm, bf16[1792,256]{1,0:T(8,128)(2,1)} %get-tuple-element.42.o_hbm, ...), custom_call_target="tpu_custom_call" | custom-call | tf_op jit(solution)/shard_map/pallas_call | solution.py:1321
  222.9 11.2 %shard_map.316 = (bf16[1792,1024]{1,0:T(8,128)(2,1)}, bf16[1792,1024]{1,0:T(8,128)(2,1)}, f32[3,128,256]{2,1,0:T(8,128)}, f32[3,128,256]{2,1,0:T(8,128)}, f32[3,...) custom-call(s32[8]{0:T(128)} %owner_ref.3, ...), custom_call_target="tpu_custom_call" | custom-call | tf_op jit(solution)/shard_map/pallas_call | solution.py:1305
